TPU v7x, 32 devices: a whole 2x2x4 slice. The times are simulated.
32 devices in a mesh: row: 8 (over z, y), col: 4 (over x, core).
Axes of the slice: x: 2, y: 2, z: 4, core: 2. Of those that a mesh axis runs over, the one named last changes fastest.
Arguments:
- features: bfloat16 [4, 1024, 128], P('col', 'row'), may hold values from -6 to 6
- weight: bfloat16 [128, 256], replicated, may hold values from -0.5 to 0.5
- tile_values: bfloat16 [8, 4, 32, 128, 128], P('row', 'col'), may hold values from -0.125 to 0.125
- tile_rows: int32 [8, 4, 32], P('row', 'col'), may hold values from 0 to 3
- tile_cols: int32 [8, 4, 32], P('row', 'col'), may hold values from 0 to 7
- tile_count: int32 [8, 4], P('row', 'col'), may hold values from 4 to 32, as said below
- cotangent: bfloat16 [8, 512, 256], P('row', 'col'), may hold values from -6 to 6
Outputs:
- output: bfloat16 [8, 512, 256], P('row', 'col')
- grad_features: bfloat16 [4, 1024, 128], P('col', 'row')
- weight_grad: float32 [128, 256], replicated
Inputs may be any that keep to these rules, and one draw needn't show every extreme that they name: Slots at or beyond a cell's tile_count are ignored; some cell is full in every draw. Tile coordinates within a cell may repeat, and repeated tiles add.
All inputs are finite; a program needn't handle non-finite values.
Results may differ from a plain program's by a relative error of at most 0.022.
Values may be sent and summed in bfloat16 or wider, within the bound.
A program may use at most 64 MiB of HBM per device.

v0:
```python
import functools

import jax
import jax.numpy as jnp
from jax import lax
from jax.experimental import pallas as pl
from jax.experimental.pallas import tpu as pltpu
from jax.sharding import PartitionSpec as P

MESH = pl.DeviceIdType.MESH
F32 = jnp.float32
BF16 = jnp.bfloat16


def fill_links(R, C, capacity, rows, cols, total, found):
    width = found.shape[1]
    lane = lax.broadcasted_iota(jnp.int32, (1, width), 1)
    count = total[0, 0]

    def key_of(t):
        return jnp.where(t < count, rows[0, 0, t] * R + cols[0, 0, t], -1)

    keys = jnp.full((1, width), -2, jnp.int32)
    for t in range(capacity):
        keys = jnp.where(lane == t, key_of(t), keys)
    before = jnp.full((1, width), capacity, jnp.int32)
    last = before
    for t in range(capacity):
        key = key_of(t)
        before = jnp.where((keys == key) & (lane > t), t, before)
        last = jnp.where(lane == key, t, last)
    found[0:1, :] = before
    found[1:2, :] = last


def kernel(
    R, C, scale,
    rows_ref, cols_ref, total_ref, feat_ref, weight_ref, tiles_ref, cot_ref,
    out_hbm, gf_hbm, wg_hbm,
    rows, cols, total_s, found, link_ref, w_ref, out_ref, gf_ref, wg_ref,
    tiles, cot, sums, dense, fbuf,
    agg_out, agg_in, gbuf, yb_out, yb_in, zb_out, zb_in,
    w1_out, w1_in, w2_out, w2_in, w3, w4,
    local_sem,
    za_s, za_r, ya_s, ya_r, ag_s, ag_r, gb_s, gb_r,
    yb_s, yb_r, zb_s, zb_r, w1_s, w1_r, w2_s, w2_r, w3_s, w3_r, w4_s, w4_r,
):
    row, col = lax.axis_index("row"), lax.axis_index("col")
    H = R // 2
    hi, lo = row // 2, row % 2
    partner = hi * 2 + (1 - lo)
    T = feat_ref.shape[1]
    capacity = tiles.shape[0]
    wrows = w4.shape[1]

    def peer(d):
        return (col + d) % C

    def z_of(k):
        return (hi + k) % H

    def z_from(k):
        return (hi + H - k) % H

    def send(src, dst, s, r, device):
        copy = pltpu.make_async_remote_copy(
            src_ref=src, dst_ref=dst, send_sem=s, recv_sem=r, device_id=device, device_id_type=MESH
        )
        copy.start()
        return copy

    def fetch(src, dst, n):
        copy = pltpu.make_async_copy(src, dst, local_sem.at[n])
        copy.start()
        return copy

    get_feat = fetch(feat_ref.at[0], fbuf.at[row], 0)
    get_ids = [fetch(rows_ref, rows, 1), fetch(cols_ref, cols, 2), fetch(total_ref, total_s, 3)]
    get_tiles = fetch(tiles_ref.at[0, 0], tiles, 4)
    get_w = fetch(weight_ref, w_ref, 5)
    get_cot = fetch(cot_ref.at[0], cot, 6)

    barrier = pltpu.get_barrier_semaphore()
    pl.semaphore_signal(barrier, inc=1, device_id=(partner, col), device_id_type=MESH)
    for k in range(1, H):
        pl.semaphore_signal(barrier, inc=1, device_id=(z_of(k) * 2 + lo, col), device_id_type=MESH)
    for d in range(1, C):
        pl.semaphore_signal(barrier, inc=1, device_id=(row, peer(d)), device_id_type=MESH)
    sums[capacity] = jnp.zeros(sums.shape[1:], F32)
    for copy in get_ids:
        copy.wait()
    fill_links(R, C, capacity, rows, cols, total_s, found)
    get_links = fetch(found, link_ref, 7)
    get_feat.wait()
    pl.semaphore_wait(barrier, 1 + (H - 1) + (C - 1))

    sent = []
    own_y = send(fbuf.at[row], fbuf.at[row], ya_s.at[0], ya_r.at[0], (partner, col))
    za = [None]
    for k in range(1, H):
        za.append(send(fbuf.at[row], fbuf.at[row], za_s.at[k], za_r.at[k], (z_of(k) * 2 + lo, col)))

    get_tiles.wait()
    get_links.wait()

    def add_slot(t, carry):
        sums[t] = tiles[t].astype(F32) + sums[link_ref[0, t]]
        return carry

    lax.fori_loop(0, capacity, add_slot, 0)

    def place(b, carry):
        i, j = b // R, b % R
        dense[pl.ds(pl.multiple_of(i * T, T), T), pl.ds(pl.multiple_of(j * T, T), T)] = sums[
            link_ref[1, b]
        ].astype(BF16)
        return carry

    lax.fori_loop(0, R * C, place, 0)

    ya = [own_y]
    for k in range(1, H):
        za[k].wait_recv()
        block = fbuf.at[z_from(k) * 2 + lo]
        ya.append(send(block, block, ya_s.at[k], ya_r.at[k], (partner, col)))
    for k in range(H):
        ya[k].wait_recv()
    sent += za[1:] + ya

    def aggregate(j):
        rows = dense[pl.ds(pl.multiple_of(j * T, T), T), :]
        return jnp.dot(rows, fbuf[...].reshape(R * T, T), preferred_element_type=F32)

    ag = []
    for d in range(1, C):
        agg_out[d - 1] = aggregate(peer(d)).astype(BF16)
        ag.append(send(agg_out.at[d - 1], agg_in.at[d - 1], ag_s.at[d - 1], ag_r.at[d - 1], (row, peer(d))))
    total = aggregate(col)
    for d in range(1, C):
        ag[d - 1].wait_recv()
        total = total + agg_in[d - 1].astype(F32)
    sent += ag
    agg = total.astype(BF16)

    get_w.wait()
    get_cot.wait()
    pre = jnp.dot(agg, w_ref[...], preferred_element_type=F32)
    sigma = jax.nn.sigmoid(pre)
    slope = sigma * (1.0 + pre * (1.0 - sigma))
    grad_pre = (cot[...].astype(F32) * slope).astype(BF16)
    gbuf[col] = lax.dot_general(
        w_ref[...], grad_pre, (((1,), (1,)), ((), ())), preferred_element_type=F32
    ).astype(BF16)
    gb = []
    for d in range(1, C):
        gb.append(send(gbuf.at[col], gbuf.at[col], gb_s.at[d - 1], gb_r.at[d - 1], (row, peer(d))))
    sent += gb

    agg_t = agg.astype(F32).T.astype(BF16)
    local = jnp.dot(agg_t, grad_pre, preferred_element_type=F32)
    half = local.shape[1] // 2
    local = jnp.concatenate([local[:, :half], local[:, half:]], axis=0)
    for c in range(C):
        w1_out[c] = local[c * wrows : (c + 1) * wrows].astype(BF16)
    w1 = []
    for d in range(1, C):
        w1.append(send(w1_out.at[peer(d)], w1_in.at[d - 1], w1_s.at[d - 1], w1_r.at[d - 1], (row, peer(d))))
    sent += w1
    out_ref[...] = (pre * sigma).astype(BF16)
    put_out = fetch(out_ref, out_hbm.at[0], 8)

    part = w1_out[col].astype(F32)
    for d in range(1, C):
        w1[d - 1].wait_recv()
        part = part + w1_in[d - 1].astype(F32)
    part = part.astype(BF16)
    w2_out[...] = part
    w2 = send(w2_out, w2_in, w2_s.at[0], w2_r.at[0], (partner, col))
    sent.append(w2)

    for d in range(1, C):
        gb[d - 1].wait_recv()
    source = jnp.concatenate([gbuf[c] for c in range(C)], axis=1)

    def back(i):
        cols = dense[:, pl.ds(pl.multiple_of(i * T, T), T)]
        return jnp.dot(source, cols, preferred_element_type=F32)

    yb = [None] * H
    for k in list(range(1, H)) + [0]:
        yb_out[k] = back(z_of(k) * 2 + (1 - lo)).astype(BF16)
        yb[k] = send(yb_out.at[k], yb_in.at[k], yb_s.at[k], yb_r.at[k], (partner, col))
    sent += yb

    w2.wait_recv()
    w3[hi] = (part.astype(F32) + w2_in[...].astype(F32)).astype(BF16)
    w3_sent = [send(w3.at[hi], w3.at[hi], w3_s.at[m], w3_r.at[m], (z_of(m) * 2 + lo, col)) for m in range(1, H)]
    zb = []
    for k in range(1, H):
        value = back(z_of(k) * 2 + lo)
        yb[k].wait_recv()
        zb_out[k] = (value + yb_in[k].astype(F32)).astype(BF16)
        zb.append(send(zb_out.at[k], zb_in.at[k], zb_s.at[k], zb_r.at[k], (z_of(k) * 2 + lo, col)))
    sent += zb + w3_sent
    mine = back(hi * 2 + lo)
    yb[0].wait_recv()
    mine = mine + yb_in[0].astype(F32)

    for copy in w3_sent:
        copy.wait_recv()
    whole = w3[0].astype(F32)
    for h in range(1, H):
        whole = whole + w3[h].astype(F32)
    w4[col] = (whole * scale).astype(BF16)
    w4_sent = [
        send(w4.at[col], w4.at[col], w4_s.at[d - 1], w4_r.at[d - 1], (row, peer(d))) for d in range(1, C)
    ]
    sent += w4_sent

    for k in range(1, H):
        zb[k - 1].wait_recv()
        mine = mine + zb_in[k].astype(F32)
    gf_ref[...] = mine.T.astype(BF16)
    put_gf = fetch(gf_ref, gf_hbm.at[0], 9)

    for copy in w4_sent:
        copy.wait_recv()
    full = w4[...].astype(F32).reshape(2, wg_ref.shape[0], half)
    wg_ref[:, :half] = full[0]
    wg_ref[:, half:] = full[1]
    put_wg = fetch(wg_ref, wg_hbm, 10)
    for copy in sent:
        copy.wait_send()
    for copy in (put_out, put_gf, put_wg):
        copy.wait()


def hand_on(a, b, c, out_a, out_b, out_c, sem):
    copies = [pltpu.make_async_copy(x, y, sem.at[n]) for n, (x, y) in enumerate([(a, out_a), (b, out_b), (c, out_c)])]
    for copy in copies:
        copy.start()
    for copy in copies:
        copy.wait()


def on_device(features, weight, tile_values, tile_rows, tile_cols, tile_count, cotangent):
    T, width = features.shape[1], features.shape[2]
    hidden = weight.shape[1]
    R, C = lax.axis_size("row"), lax.axis_size("col")
    H = R // 2
    capacity = tile_values.shape[2]
    scale = (T * R * C) ** (-0.5)
    wrows = 2 * width // C
    width_links = -(-max(capacity, R * C) // 128) * 128
    hbm = pl.BlockSpec(memory_space=pltpu.HBM)

    def dma(n):
        return pltpu.SemaphoreType.DMA((n,))

    outs = (
        jax.ShapeDtypeStruct((1, T, hidden), BF16),
        jax.ShapeDtypeStruct((1, T, width), BF16),
        jax.ShapeDtypeStruct((width, hidden), F32),
    )
    results = pl.pallas_call(
        functools.partial(kernel, R, C, scale),
        out_shape=outs,
        in_specs=[hbm] * 7,
        out_specs=(hbm,) * 3,
        scratch_shapes=[
            pltpu.SMEM((1, 1, capacity), jnp.int32),
            pltpu.SMEM((1, 1, capacity), jnp.int32),
            pltpu.SMEM((1, 1), jnp.int32),
            pltpu.VMEM((2, width_links), jnp.int32),
            pltpu.SMEM((2, width_links), jnp.int32),
            pltpu.VMEM((width, hidden), BF16),
            pltpu.VMEM((T, hidden), BF16),
            pltpu.VMEM((T, width), BF16),
            pltpu.VMEM((width, hidden), F32),
            pltpu.VMEM((capacity, T, T), BF16),
            pltpu.VMEM((T, hidden), BF16),
            pltpu.VMEM((capacity + 1, T, T), F32),
            pltpu.VMEM((C * T, R * T), BF16),
            pltpu.VMEM((R, T, width), BF16),
            pltpu.VMEM((C - 1, T, width), BF16),
            pltpu.VMEM((C - 1, T, width), BF16),
            pltpu.VMEM((C, width, T), BF16),
            pltpu.VMEM((H, width, T), BF16),
            pltpu.VMEM((H, width, T), BF16),
            pltpu.VMEM((H, width, T), BF16),
            pltpu.VMEM((H, width, T), BF16),
            pltpu.VMEM((C, wrows, hidden // 2), BF16),
            pltpu.VMEM((C - 1, wrows, hidden // 2), BF16),
            pltpu.VMEM((wrows, hidden // 2), BF16),
            pltpu.VMEM((wrows, hidden // 2), BF16),
            pltpu.VMEM((H, wrows, hidden // 2), BF16),
            pltpu.VMEM((C, wrows, hidden // 2), BF16),
            dma(11),
            dma(H), dma(H), dma(H), dma(H), dma(C - 1), dma(C - 1), dma(C - 1), dma(C - 1),
            dma(H), dma(H), dma(H), dma(H), dma(C - 1), dma(C - 1), dma(1), dma(1),
            dma(H), dma(H), dma(C - 1), dma(C - 1),
        ],
        compiler_params=pltpu.CompilerParams(
            collective_id=0, has_side_effects=True, vmem_limit_bytes=60 * 1024 * 1024
        ),
    )(tile_rows, tile_cols, tile_count, features, weight, tile_values, cotangent)
    return pl.pallas_call(
        hand_on,
        out_shape=outs,
        in_specs=[hbm] * 3,
        out_specs=(hbm,) * 3,
        scratch_shapes=[dma(3)],
        compiler_params=pltpu.CompilerParams(vmem_limit_bytes=60 * 1024 * 1024),
    )(*results)


def solution(mesh):
    placed = (
        P("col", "row", None),
        P(),
        P("row", "col", None, None, None),
        P("row", "col", None),
        P("row", "col", None),
        P("row", "col"),
        P("row", "col", None),
    )
    return jax.shard_map(
        on_device,
        mesh=mesh,
        in_specs=placed,
        out_specs=(P("row", "col", None), P("col", "row", None), P()),
        check_vma=False,
    )
```

profile of v0, /device:TPU:0, one launch (start us, length us, event | category | flops | bytes accessed | tf_op | source)
XLA Modules:
  0.0 41.3 jit_solution(7158649082973106730)
XLA Ops:
  1.3 31.9 %shard_map.94 = (bf16[1,128,256]{2,1,0:T(8,128)(2,1)}, bf16[1,128,128]{2,1,0:T(8,128)(2,1)}, f32[128,256]{1,0:T(8,128)}) custom-call(s32[1,1,32]{2,1,0:T(1,128)} %rows_ref.1, s32[1,1,32]{2,1,0:T(1,128)} %cols_ref.1, s32[1,1]{1,0:T(1,128)S(6)} %copy.10.total_ref, bf16[1,128,128]{2,1,0:T(8,128)(2,1)} %feat_ref.1, bf16[128,256]{1,0:T(8,128)(2,1)} %weight_ref.1, ...), custom_call_target="tpu_custom_call" | custom-call | tf_op jit(solution)/shard_map/pallas_call | solution.py:265
  33.2 8.1 %shard_map.95 = (bf16[1,128,256]{2,1,0:T(8,128)(2,1)}, bf16[1,128,128]{2,1,0:T(8,128)(2,1)}, f32[128,256]{1,0:T(8,128)}) custom-call(bf16[1,128,256]{2,1,0:T(8,128)(2,1)} %get-tuple-element.6.a, bf16[1,128,128]{2,1,0:T(8,128)(2,1)} %get-tuple-element.7.b, f32[128,256]{1,0:T(8,128)} %get-tuple-element.8.c), custom_call_target="tpu_custom_call" | custom-call | tf_op jit(solution)/shard_map/pallas_call | solution.py:307
where the time goes:
time: 41.4 us; the launch traced here: 41.3 us
  Pallas kernels  40 us (97%)
  between operations  1.29 us (3%)
    pallas_call x1, Pallas kernels, on_device(): pl.pallas_call(functools.partial(kernel, R, C, scale), out_shape=outs, in...  31.9 us
    pallas_call x1, Pallas kernels, on_device(): pl.pallas_call(hand_on, out_shape=outs, in_specs=[hbm] * 3, out_specs=(hb...  8.08 us

commit v1 on v0

--- a/solution.py
+++ b/solution.py
@@ -57,10 +57,12 @@
         return (col + d) % C
 
     def z_of(k):
-        return (hi + k) % H
-
-    def z_from(k):
-        return (hi + H - k) % H
+        other, bit = hi, 1
+        while bit < H:
+            if k & bit:
+                other = other + bit * (1 - 2 * ((hi // bit) % 2))
+            bit *= 2
+        return other
 
     def send(src, dst, s, r, device):
         copy = pltpu.make_async_remote_copy(
@@ -86,20 +88,20 @@
         pl.semaphore_signal(barrier, inc=1, device_id=(z_of(k) * 2 + lo, col), device_id_type=MESH)
     for d in range(1, C):
         pl.semaphore_signal(barrier, inc=1, device_id=(row, peer(d)), device_id_type=MESH)
+    get_feat.wait()
+    pl.semaphore_wait(barrier, 1 + (H - 1) + (C - 1))
+
+    sent = []
+    own_y = send(fbuf.at[row], fbuf.at[row], ya_s.at[0], ya_r.at[0], (partner, col))
+    za = [None]
+    for k in range(1, H):
+        za.append(send(fbuf.at[row], fbuf.at[row], za_s.at[k], za_r.at[k], (z_of(k) * 2 + lo, col)))
+
     sums[capacity] = jnp.zeros(sums.shape[1:], F32)
     for copy in get_ids:
         copy.wait()
     fill_links(R, C, capacity, rows, cols, total_s, found)
     get_links = fetch(found, link_ref, 7)
-    get_feat.wait()
-    pl.semaphore_wait(barrier, 1 + (H - 1) + (C - 1))
-
-    sent = []
-    own_y = send(fbuf.at[row], fbuf.at[row], ya_s.at[0], ya_r.at[0], (partner, col))
-    za = [None]
-    for k in range(1, H):
-        za.append(send(fbuf.at[row], fbuf.at[row], za_s.at[k], za_r.at[k], (z_of(k) * 2 + lo, col)))
-
     get_tiles.wait()
     get_links.wait()
 
@@ -107,7 +109,16 @@
         sums[t] = tiles[t].astype(F32) + sums[link_ref[0, t]]
         return carry
 
-    lax.fori_loop(0, capacity, add_slot, 0)
+    lax.fori_loop(0, capacity, add_slot, 0, unroll=2)
+
+    ya = [own_y]
+
+    def forward(k):
+        za[k].wait_recv()
+        block = fbuf.at[z_of(k) * 2 + lo]
+        ya.append(send(block, block, ya_s.at[k], ya_r.at[k], (partner, col)))
+
+    forward(1)
 
     def place(b, carry):
         i, j = b // R, b % R
@@ -116,13 +127,10 @@
         ].astype(BF16)
         return carry
 
-    lax.fori_loop(0, R * C, place, 0)
-
-    ya = [own_y]
-    for k in range(1, H):
-        za[k].wait_recv()
-        block = fbuf.at[z_from(k) * 2 + lo]
-        ya.append(send(block, block, ya_s.at[k], ya_r.at[k], (partner, col)))
+    lax.fori_loop(0, R * C, place, 0, unroll=4)
+
+    for k in range(2, H):
+        forward(k)
     for k in range(H):
         ya[k].wait_recv()
     sent += za[1:] + ya
@@ -187,7 +195,8 @@
         return jnp.dot(source, cols, preferred_element_type=F32)
 
     yb = [None] * H
-    for k in list(range(1, H)) + [0]:
+    far = list(range(2, H)) + [1]
+    for k in far + [0]:
         yb_out[k] = back(z_of(k) * 2 + (1 - lo)).astype(BF16)
         yb[k] = send(yb_out.at[k], yb_in.at[k], yb_s.at[k], yb_r.at[k], (partner, col))
     sent += yb
@@ -196,7 +205,7 @@
     w3[hi] = (part.astype(F32) + w2_in[...].astype(F32)).astype(BF16)
     w3_sent = [send(w3.at[hi], w3.at[hi], w3_s.at[m], w3_r.at[m], (z_of(m) * 2 + lo, col)) for m in range(1, H)]
     zb = []
-    for k in range(1, H):
+    for k in far:
         value = back(z_of(k) * 2 + lo)
         yb[k].wait_recv()
         zb_out[k] = (value + yb_in[k].astype(F32)).astype(BF16)
@@ -217,8 +226,9 @@
     ]
     sent += w4_sent
 
+    for copy in zb:
+        copy.wait_recv()
     for k in range(1, H):
-        zb[k - 1].wait_recv()
         mine = mine + zb_in[k].astype(F32)
     gf_ref[...] = mine.T.astype(BF16)
     put_gf = fetch(gf_ref, gf_hbm.at[0], 9)
@@ -235,14 +245,6 @@
         copy.wait()
 
 
-def hand_on(a, b, c, out_a, out_b, out_c, sem):
-    copies = [pltpu.make_async_copy(x, y, sem.at[n]) for n, (x, y) in enumerate([(a, out_a), (b, out_b), (c, out_c)])]
-    for copy in copies:
-        copy.start()
-    for copy in copies:
-        copy.wait()
-
-
 def on_device(features, weight, tile_values, tile_rows, tile_cols, tile_count, cotangent):
     T, width = features.shape[1], features.shape[2]
     hidden = weight.shape[1]
@@ -262,7 +264,7 @@
         jax.ShapeDtypeStruct((1, T, width), BF16),
         jax.ShapeDtypeStruct((width, hidden), F32),
     )
-    results = pl.pallas_call(
+    return pl.pallas_call(
         functools.partial(kernel, R, C, scale),
         out_shape=outs,
         in_specs=[hbm] * 7,
@@ -304,14 +306,6 @@
             collective_id=0, has_side_effects=True, vmem_limit_bytes=60 * 1024 * 1024
         ),
     )(tile_rows, tile_cols, tile_count, features, weight, tile_values, cotangent)
-    return pl.pallas_call(
-        hand_on,
-        out_shape=outs,
-        in_specs=[hbm] * 3,
-        out_specs=(hbm,) * 3,
-        scratch_shapes=[dma(3)],
-        compiler_params=pltpu.CompilerParams(vmem_limit_bytes=60 * 1024 * 1024),
-    )(*results)
 
 
 def solution(mesh):

time: 41.4 us -> 37.2 us (0.90)
  Pallas kernels: 40 us -> 32.1 us
  local copies, waits for them, and re-layouts: 0 us -> 3.54 us
    pallas_call x1 -> x0, Pallas kernels: 8.08 us -> none  [on_device(): pl.pallas_call(hand_on, out_shape=outs, in_specs=[hbm] * 3, out_specs=(hb...]
    unnamed x0 -> x5, local copies, waits for them, and re-layouts: none -> 3.54 us
where the time goes in v1:
time: 37.2 us; the launch traced here: 36.9 us
  Pallas kernels  32.1 us (86%)
  local copies, waits for them, and re-layouts  3.54 us (10%)
  between operations  1.3 us (3%)
    pallas_call x1, Pallas kernels, on_device(): pl.pallas_call(functools.partial(kernel, R, C, scale), out_shape=outs, in...  32.1 us
    unnamed x5, local copies, waits for them, and re-layouts  3.54 us

profile of v1, /device:TPU:0, one launch (start us, length us, event | category | flops | bytes accessed | tf_op | source)
XLA Modules:
  0.0 36.9 jit_solution(14904255702825067595)
XLA Ops:
  1.3 32.1 %shard_map.94 = (bf16[1,128,256]{2,1,0:T(8,128)(2,1)}, bf16[1,128,128]{2,1,0:T(8,128)(2,1)}, f32[128,256]{1,0:T(8,128)}) custom-call(s32[1,1,32]{2,1,0:T(1,128)} %rows_ref.1, s32[1,1,32]{2,1,0:T(1,128)} %cols_ref.1, s32[1,1]{1,0:T(1,128)S(6)} %copy.13.total_ref, bf16[1,128,128]{2,1,0:T(8,128)(2,1)} %feat_ref.1, bf16[128,256]{1,0:T(8,128)(2,1)} %weight_ref.1, ...), custom_call_target="tpu_custom_call" | custom-call | tf_op jit(solution)/shard_map/pallas_call | solution.py:267
  33.4 0.0 copy-start
  33.4 1.5 %copy.14 = bf16[1,128,256]{2,1,0:T(8,128)(2,1)} copy(bf16[1,128,256]{2,1,0:T(8,128)(2,1)} %get-tuple-element.6) | data formatting | bytes 131072
  34.9 1.4 %copy.15 = bf16[1,128,128]{2,1,0:T(8,128)(2,1)} copy(bf16[1,128,128]{2,1,0:T(8,128)(2,1)} %get-tuple-element.7) | data formatting | bytes 65536
  36.3 0.0 copy-done
  36.3 0.7 %copy.16 = f32[128,256]{1,0:T(8,128)} copy(f32[128,256]{1,0:T(8,128)S(1)} %copy-done) | data formatting | bytes 262144
Async XLA Ops:
  33.4 2.9 %copy-start = (f32[128,256]{1,0:T(8,128)S(1)}, f32[128,256]{1,0:T(8,128)}, u32[]{:S(2)}) copy-start(f32[128,256]{1,0:T(8,128)} %get-tuple-element.8) | copy-start | bytes 393220

commit v2 on v1

--- a/solution.py
+++ b/solution.py
@@ -102,15 +102,6 @@
         copy.wait()
     fill_links(R, C, capacity, rows, cols, total_s, found)
     get_links = fetch(found, link_ref, 7)
-    get_tiles.wait()
-    get_links.wait()
-
-    def add_slot(t, carry):
-        sums[t] = tiles[t].astype(F32) + sums[link_ref[0, t]]
-        return carry
-
-    lax.fori_loop(0, capacity, add_slot, 0, unroll=2)
-
     ya = [own_y]
 
     def forward(k):
@@ -119,6 +110,17 @@
         ya.append(send(block, block, ya_s.at[k], ya_r.at[k], (partner, col)))
 
     forward(1)
+    get_tiles.wait()
+    get_links.wait()
+
+    def add_slot(t, carry):
+        sums[t] = tiles[t].astype(F32) + sums[link_ref[0, t]]
+        return carry
+
+    lax.fori_loop(0, capacity, add_slot, 0, unroll=2)
+
+    for k in range(2, min(3, H)):
+        forward(k)
 
     def place(b, carry):
         i, j = b // R, b % R
@@ -129,7 +131,7 @@
 
     lax.fori_loop(0, R * C, place, 0, unroll=4)
 
-    for k in range(2, H):
+    for k in range(3, H):
         forward(k)
     for k in range(H):
         ya[k].wait_recv()
@@ -174,9 +176,26 @@
     for d in range(1, C):
         w1.append(send(w1_out.at[peer(d)], w1_in.at[d - 1], w1_s.at[d - 1], w1_r.at[d - 1], (row, peer(d))))
     sent += w1
-    out_ref[...] = (pre * sigma).astype(BF16)
-    put_out = fetch(out_ref, out_hbm.at[0], 8)
-
+    out_ref[0] = (pre * sigma).astype(BF16)
+    put_out = fetch(out_ref, out_hbm, 8)
+
+    for d in range(1, C):
+        gb[d - 1].wait_recv()
+    source = jnp.concatenate([gbuf[c] for c in range(C)], axis=1)
+
+    def back(i):
+        cols = dense[:, pl.ds(pl.multiple_of(i * T, T), T)]
+        return jnp.dot(source, cols, preferred_element_type=F32)
+
+    yb = [None] * H
+    far = list(range(2, H)) + [1]
+
+    def back_y(k):
+        yb_out[k] = back(z_of(k) * 2 + (1 - lo)).astype(BF16)
+        yb[k] = send(yb_out.at[k], yb_in.at[k], yb_s.at[k], yb_r.at[k], (partner, col))
+
+    for k in far[:2]:
+        back_y(k)
     part = w1_out[col].astype(F32)
     for d in range(1, C):
         w1[d - 1].wait_recv()
@@ -186,30 +205,24 @@
     w2 = send(w2_out, w2_in, w2_s.at[0], w2_r.at[0], (partner, col))
     sent.append(w2)
 
-    for d in range(1, C):
-        gb[d - 1].wait_recv()
-    source = jnp.concatenate([gbuf[c] for c in range(C)], axis=1)
-
-    def back(i):
-        cols = dense[:, pl.ds(pl.multiple_of(i * T, T), T)]
-        return jnp.dot(source, cols, preferred_element_type=F32)
-
-    yb = [None] * H
-    far = list(range(2, H)) + [1]
-    for k in far + [0]:
-        yb_out[k] = back(z_of(k) * 2 + (1 - lo)).astype(BF16)
-        yb[k] = send(yb_out.at[k], yb_in.at[k], yb_s.at[k], yb_r.at[k], (partner, col))
+    for k in far[2:] + [0]:
+        back_y(k)
     sent += yb
 
-    w2.wait_recv()
-    w3[hi] = (part.astype(F32) + w2_in[...].astype(F32)).astype(BF16)
-    w3_sent = [send(w3.at[hi], w3.at[hi], w3_s.at[m], w3_r.at[m], (z_of(m) * 2 + lo, col)) for m in range(1, H)]
     zb = []
-    for k in far:
+
+    def back_z(k):
         value = back(z_of(k) * 2 + lo)
         yb[k].wait_recv()
         zb_out[k] = (value + yb_in[k].astype(F32)).astype(BF16)
         zb.append(send(zb_out.at[k], zb_in.at[k], zb_s.at[k], zb_r.at[k], (z_of(k) * 2 + lo, col)))
+
+    back_z(far[0])
+    w2.wait_recv()
+    w3[hi] = (part.astype(F32) + w2_in[...].astype(F32)).astype(BF16)
+    w3_sent = [send(w3.at[hi], w3.at[hi], w3_s.at[m], w3_r.at[m], (z_of(m) * 2 + lo, col)) for m in range(1, H)]
+    for k in far[1:]:
+        back_z(k)
     sent += zb + w3_sent
     mine = back(hi * 2 + lo)
     yb[0].wait_recv()
@@ -230,8 +243,8 @@
         copy.wait_recv()
     for k in range(1, H):
         mine = mine + zb_in[k].astype(F32)
-    gf_ref[...] = mine.T.astype(BF16)
-    put_gf = fetch(gf_ref, gf_hbm.at[0], 9)
+    gf_ref[0] = mine.T.astype(BF16)
+    put_gf = fetch(gf_ref, gf_hbm, 9)
 
     for copy in w4_sent:
         copy.wait_recv()
@@ -245,6 +258,19 @@
         copy.wait()
 
 
+def hand_on(*refs):
+    sources, targets, held, sem = refs[:3], refs[3:6], refs[6:9], refs[9]
+    reads = [pltpu.make_async_copy(sources[n], held[n], sem.at[n]) for n in range(3)]
+    writes = [pltpu.make_async_copy(held[n], targets[n], sem.at[3 + n]) for n in range(3)]
+    for copy in reads:
+        copy.start()
+    for read, write in zip(reads, writes):
+        read.wait()
+        write.start()
+    for copy in writes:
+        copy.wait()
+
+
 def on_device(features, weight, tile_values, tile_rows, tile_cols, tile_count, cotangent):
     T, width = features.shape[1], features.shape[2]
     hidden = weight.shape[1]
@@ -264,7 +290,7 @@
         jax.ShapeDtypeStruct((1, T, width), BF16),
         jax.ShapeDtypeStruct((width, hidden), F32),
     )
-    return pl.pallas_call(
+    results = pl.pallas_call(
         functools.partial(kernel, R, C, scale),
         out_shape=outs,
         in_specs=[hbm] * 7,
@@ -276,9 +302,7 @@
             pltpu.VMEM((2, width_links), jnp.int32),
             pltpu.SMEM((2, width_links), jnp.int32),
             pltpu.VMEM((width, hidden), BF16),
-            pltpu.VMEM((T, hidden), BF16),
-            pltpu.VMEM((T, width), BF16),
-            pltpu.VMEM((width, hidden), F32),
+            *[pltpu.VMEM(o.shape, o.dtype) for o in outs],
             pltpu.VMEM((capacity, T, T), BF16),
             pltpu.VMEM((T, hidden), BF16),
             pltpu.VMEM((capacity + 1, T, T), F32),
@@ -306,6 +330,14 @@
             collective_id=0, has_side_effects=True, vmem_limit_bytes=60 * 1024 * 1024
         ),
     )(tile_rows, tile_cols, tile_count, features, weight, tile_values, cotangent)
+    return pl.pallas_call(
+        hand_on,
+        out_shape=outs,
+        in_specs=[hbm] * 3,
+        out_specs=(hbm,) * 3,
+        scratch_shapes=[*[pltpu.VMEM(o.shape, o.dtype) for o in outs], dma(6)],
+        compiler_params=pltpu.CompilerParams(vmem_limit_bytes=60 * 1024 * 1024),
+    )(*results)
 
 
 def solution(mesh):

time: 37.2 us -> 36.1 us (0.970)
  local copies, waits for them, and re-layouts: 3.54 us -> 0 us
  Pallas kernels: 32.1 us -> 34.7 us
    unnamed x5 -> x0, local copies, waits for them, and re-layouts: 3.54 us -> none
    pallas_call x0 -> x1, Pallas kernels: none -> 1.67 us  [on_device(): pl.pallas_call(hand_on, out_shape=outs, in_specs=[hbm] * 3, out_specs=(hb...]
    pallas_call x1, Pallas kernels: 32.1 us -> 33 us  [on_device(): pl.pallas_call(functools.partial(kernel, R, C, scale), out_shape=outs, in...]
where the time goes in v2:
time: 36.1 us; the launch traced here: 36 us
  Pallas kernels  34.7 us (96%)
  between operations  1.29 us (4%)
    pallas_call x1, Pallas kernels, on_device(): pl.pallas_call(functools.partial(kernel, R, C, scale), out_shape=outs, in...  33 us
    pallas_call x1, Pallas kernels, on_device(): pl.pallas_call(hand_on, out_shape=outs, in_specs=[hbm] * 3, out_specs=(hb...  1.67 us

profile of v2, /device:TPU:0, one launch (start us, length us, event | category | flops | bytes accessed | tf_op | source)
XLA Modules:
  0.0 36.0 jit_solution(15554470307824074559)
XLA Ops:
  1.3 33.0 %shard_map.94 = (bf16[1,128,256]{2,1,0:T(8,128)(2,1)}, bf16[1,128,128]{2,1,0:T(8,128)(2,1)}, f32[128,256]{1,0:T(8,128)}) custom-call(s32[1,1,32]{2,1,0:T(1,128)} %rows_ref.1, s32[1,1,32]{2,1,0:T(1,128)} %cols_ref.1, s32[1,1]{1,0:T(1,128)S(6)} %copy.10.total_ref, bf16[1,128,128]{2,1,0:T(8,128)(2,1)} %feat_ref.1, bf16[128,256]{1,0:T(8,128)(2,1)} %weight_ref.1, ...), custom_call_target="tpu_custom_call" | custom-call | tf_op jit(solution)/shard_map/pallas_call | solution.py:293
  34.3 1.7 %shard_map.95 = (bf16[1,128,256]{2,1,0:T(8,128)(2,1)}, bf16[1,128,128]{2,1,0:T(8,128)(2,1)}, f32[128,256]{1,0:T(8,128)}) custom-call(bf16[1,128,256]{2,1,0:T(8,128)(2,1)} %get-tuple-element.6.refs_0_, bf16[1,128,128]{2,1,0:T(8,128)(2,1)} %get-tuple-element.7.refs_1_, f32[128,256]{1,0:T(8,128)} %get-tuple-element.8.refs_2_), custom_call_target="tpu_custom_call" | custom-call | tf_op jit(solution)/shard_map/pallas_call | solution.py:333

commit v3 on v2

--- a/solution.py
+++ b/solution.py
@@ -40,10 +40,10 @@
     rows, cols, total_s, found, link_ref, w_ref, out_ref, gf_ref, wg_ref,
     tiles, cot, sums, dense, fbuf,
     agg_out, agg_in, gbuf, yb_out, yb_in, zb_out, zb_in,
-    w1_out, w1_in, w2_out, w2_in, w3, w4,
+    w1_out, w1_in, w3, w4,
     local_sem,
     za_s, za_r, ya_s, ya_r, ag_s, ag_r, gb_s, gb_r,
-    yb_s, yb_r, zb_s, zb_r, w1_s, w1_r, w2_s, w2_r, w3_s, w3_r, w4_s, w4_r,
+    yb_s, yb_r, zb_s, zb_r, w1_s, w1_r, w3_s, w3_r, w4_s, w4_r,
 ):
     row, col = lax.axis_index("row"), lax.axis_index("col")
     H = R // 2
@@ -83,13 +83,12 @@
     get_cot = fetch(cot_ref.at[0], cot, 6)
 
     barrier = pltpu.get_barrier_semaphore()
-    pl.semaphore_signal(barrier, inc=1, device_id=(partner, col), device_id_type=MESH)
-    for k in range(1, H):
-        pl.semaphore_signal(barrier, inc=1, device_id=(z_of(k) * 2 + lo, col), device_id_type=MESH)
+    for n in range(1, R):
+        pl.semaphore_signal(barrier, inc=1, device_id=((row + n) % R, col), device_id_type=MESH)
     for d in range(1, C):
         pl.semaphore_signal(barrier, inc=1, device_id=(row, peer(d)), device_id_type=MESH)
     get_feat.wait()
-    pl.semaphore_wait(barrier, 1 + (H - 1) + (C - 1))
+    pl.semaphore_wait(barrier, (R - 1) + (C - 1))
 
     sent = []
     own_y = send(fbuf.at[row], fbuf.at[row], ya_s.at[0], ya_r.at[0], (partner, col))
@@ -109,7 +108,6 @@
         block = fbuf.at[z_of(k) * 2 + lo]
         ya.append(send(block, block, ya_s.at[k], ya_r.at[k], (partner, col)))
 
-    forward(1)
     get_tiles.wait()
     get_links.wait()
 
@@ -119,8 +117,7 @@
 
     lax.fori_loop(0, capacity, add_slot, 0, unroll=2)
 
-    for k in range(2, min(3, H)):
-        forward(k)
+    forward(1)
 
     def place(b, carry):
         i, j = b // R, b % R
@@ -131,7 +128,7 @@
 
     lax.fori_loop(0, R * C, place, 0, unroll=4)
 
-    for k in range(3, H):
+    for k in range(2, H):
         forward(k)
     for k in range(H):
         ya[k].wait_recv()
@@ -183,6 +180,15 @@
         gb[d - 1].wait_recv()
     source = jnp.concatenate([gbuf[c] for c in range(C)], axis=1)
 
+    part = w1_out[col].astype(F32)
+    for d in range(1, C):
+        w1[d - 1].wait_recv()
+        part = part + w1_in[d - 1].astype(F32)
+    w3[row] = part.astype(BF16)
+    w3_sent = [
+        send(w3.at[row], w3.at[row], w3_s.at[n], w3_r.at[n], ((row + n) % R, col)) for n in range(1, R)
+    ]
+
     def back(i):
         cols = dense[:, pl.ds(pl.multiple_of(i * T, T), T)]
         return jnp.dot(source, cols, preferred_element_type=F32)
@@ -194,18 +200,7 @@
         yb_out[k] = back(z_of(k) * 2 + (1 - lo)).astype(BF16)
         yb[k] = send(yb_out.at[k], yb_in.at[k], yb_s.at[k], yb_r.at[k], (partner, col))
 
-    for k in far[:2]:
-        back_y(k)
-    part = w1_out[col].astype(F32)
-    for d in range(1, C):
-        w1[d - 1].wait_recv()
-        part = part + w1_in[d - 1].astype(F32)
-    part = part.astype(BF16)
-    w2_out[...] = part
-    w2 = send(w2_out, w2_in, w2_s.at[0], w2_r.at[0], (partner, col))
-    sent.append(w2)
-
-    for k in far[2:] + [0]:
+    for k in far + [0]:
         back_y(k)
     sent += yb
 
@@ -218,26 +213,23 @@
         zb.append(send(zb_out.at[k], zb_in.at[k], zb_s.at[k], zb_r.at[k], (z_of(k) * 2 + lo, col)))
 
     back_z(far[0])
-    w2.wait_recv()
-    w3[hi] = (part.astype(F32) + w2_in[...].astype(F32)).astype(BF16)
-    w3_sent = [send(w3.at[hi], w3.at[hi], w3_s.at[m], w3_r.at[m], (z_of(m) * 2 + lo, col)) for m in range(1, H)]
+    for copy in w3_sent:
+        copy.wait_recv()
+    whole = w3[0].astype(F32)
+    for h in range(1, R):
+        whole = whole + w3[h].astype(F32)
+    w4[col] = (whole * scale).astype(BF16)
+    w4_sent = [
+        send(w4.at[col], w4.at[col], w4_s.at[d - 1], w4_r.at[d - 1], (row, peer(d))) for d in range(1, C)
+    ]
+    sent += w4_sent
+
     for k in far[1:]:
         back_z(k)
     sent += zb + w3_sent
     mine = back(hi * 2 + lo)
     yb[0].wait_recv()
     mine = mine + yb_in[0].astype(F32)
-
-    for copy in w3_sent:
-        copy.wait_recv()
-    whole = w3[0].astype(F32)
-    for h in range(1, H):
-        whole = whole + w3[h].astype(F32)
-    w4[col] = (whole * scale).astype(BF16)
-    w4_sent = [
-        send(w4.at[col], w4.at[col], w4_s.at[d - 1], w4_r.at[d - 1], (row, peer(d))) for d in range(1, C)
-    ]
-    sent += w4_sent
 
     for copy in zb:
         copy.wait_recv()
@@ -317,14 +309,12 @@
             pltpu.VMEM((H, width, T), BF16),
             pltpu.VMEM((C, wrows, hidden // 2), BF16),
             pltpu.VMEM((C - 1, wrows, hidden // 2), BF16),
-            pltpu.VMEM((wrows, hidden // 2), BF16),
-            pltpu.VMEM((wrows, hidden // 2), BF16),
-            pltpu.VMEM((H, wrows, hidden // 2), BF16),
+            pltpu.VMEM((R, wrows, hidden // 2), BF16),
             pltpu.VMEM((C, wrows, hidden // 2), BF16),
             dma(11),
             dma(H), dma(H), dma(H), dma(H), dma(C - 1), dma(C - 1), dma(C - 1), dma(C - 1),
-            dma(H), dma(H), dma(H), dma(H), dma(C - 1), dma(C - 1), dma(1), dma(1),
-            dma(H), dma(H), dma(C - 1), dma(C - 1),
+            dma(H), dma(H), dma(H), dma(H), dma(C - 1), dma(C - 1),
+            dma(R), dma(R), dma(C - 1), dma(C - 1),
         ],
         compiler_params=pltpu.CompilerParams(
             collective_id=0, has_side_effects=True, vmem_limit_bytes=60 * 1024 * 1024

time: 36.1 us -> 34.8 us (0.964)
  Pallas kernels: 34.7 us -> 33.4 us
    pallas_call x1, Pallas kernels: 33 us -> 31.7 us  [on_device(): pl.pallas_call(functools.partial(kernel, R, C, scale), out_shape=outs, in...]
where the time goes in v3:
time: 34.8 us; the launch traced here: 34.7 us
  Pallas kernels  33.4 us (96%)
  between operations  1.29 us (4%)
    pallas_call x1, Pallas kernels, on_device(): pl.pallas_call(functools.partial(kernel, R, C, scale), out_shape=outs, in...  31.7 us
    pallas_call x1, Pallas kernels, on_device(): pl.pallas_call(hand_on, out_shape=outs, in_specs=[hbm] * 3, out_specs=(hb...  1.67 us

profile of v3, /device:TPU:0, one launch (start us, length us, event | category | flops | bytes accessed | tf_op | source)
XLA Modules:
  0.0 34.7 jit_solution(2359285227176476924)
XLA Ops:
  1.3 31.7 %shard_map.94 = (bf16[1,128,256]{2,1,0:T(8,128)(2,1)}, bf16[1,128,128]{2,1,0:T(8,128)(2,1)}, f32[128,256]{1,0:T(8,128)}) custom-call(s32[1,1,32]{2,1,0:T(1,128)} %rows_ref.1, s32[1,1,32]{2,1,0:T(1,128)} %cols_ref.1, s32[1,1]{1,0:T(1,128)S(6)} %copy.10.total_ref, bf16[1,128,128]{2,1,0:T(8,128)(2,1)} %feat_ref.1, bf16[128,256]{1,0:T(8,128)(2,1)} %weight_ref.1, ...), custom_call_target="tpu_custom_call" | custom-call | tf_op jit(solution)/shard_map/pallas_call | solution.py:285
  33.0 1.7 %shard_map.95 = (bf16[1,128,256]{2,1,0:T(8,128)(2,1)}, bf16[1,128,128]{2,1,0:T(8,128)(2,1)}, f32[128,256]{1,0:T(8,128)}) custom-call(bf16[1,128,256]{2,1,0:T(8,128)(2,1)} %get-tuple-element.6.refs_0_, bf16[1,128,128]{2,1,0:T(8,128)(2,1)} %get-tuple-element.7.refs_1_, f32[128,256]{1,0:T(8,128)} %get-tuple-element.8.refs_2_), custom_call_target="tpu_custom_call" | custom-call | tf_op jit(solution)/shard_map/pallas_call | solution.py:323

commit v4 on v3

--- a/solution.py
+++ b/solution.py
@@ -96,12 +96,14 @@
     for k in range(1, H):
         za.append(send(fbuf.at[row], fbuf.at[row], za_s.at[k], za_r.at[k], (z_of(k) * 2 + lo, col)))
 
+    near = send(fbuf.at[row], fbuf.at[row], ya_s.at[1], ya_r.at[1], (z_of(1) * 2 + 1 - lo, col))
+
     sums[capacity] = jnp.zeros(sums.shape[1:], F32)
     for copy in get_ids:
         copy.wait()
     fill_links(R, C, capacity, rows, cols, total_s, found)
     get_links = fetch(found, link_ref, 7)
-    ya = [own_y]
+    ya = [own_y, near]
 
     def forward(k):
         za[k].wait_recv()
@@ -117,7 +119,6 @@
 
     lax.fori_loop(0, capacity, add_slot, 0, unroll=2)
 
-    forward(1)
 
     def place(b, carry):
         i, j = b // R, b % R
@@ -130,6 +131,7 @@
 
     for k in range(2, H):
         forward(k)
+    za[1].wait_recv()
     for k in range(H):
         ya[k].wait_recv()
     sent += za[1:] + ya

time: 34.8 us -> 35 us (level)
  no operation moved by 1% of the time
where the time goes in v4:
time: 35 us; the launch traced here: 34.8 us
  Pallas kernels  33.6 us (96%)
  between operations  1.29 us (4%)
    pallas_call x1, Pallas kernels, on_device(): pl.pallas_call(functools.partial(kernel, R, C, scale), out_shape=outs, in...  31.9 us
    pallas_call x1, Pallas kernels, on_device(): pl.pallas_call(hand_on, out_shape=outs, in_specs=[hbm] * 3, out_specs=(hb...  1.67 us

profile of v4, /device:TPU:0, one launch (start us, length us, event | category | flops | bytes accessed | tf_op | source)
XLA Modules:
  0.0 34.8 jit_solution(15529175695183503108)
XLA Ops:
  1.3 31.9 %shard_map.94 = (bf16[1,128,256]{2,1,0:T(8,128)(2,1)}, bf16[1,128,128]{2,1,0:T(8,128)(2,1)}, f32[128,256]{1,0:T(8,128)}) custom-call(s32[1,1,32]{2,1,0:T(1,128)} %rows_ref.1, s32[1,1,32]{2,1,0:T(1,128)} %cols_ref.1, s32[1,1]{1,0:T(1,128)S(6)} %copy.10.total_ref, bf16[1,128,128]{2,1,0:T(8,128)(2,1)} %feat_ref.1, bf16[128,256]{1,0:T(8,128)(2,1)} %weight_ref.1, ...), custom_call_target="tpu_custom_call" | custom-call | tf_op jit(solution)/shard_map/pallas_call | solution.py:287
  33.2 1.7 %shard_map.95 = (bf16[1,128,256]{2,1,0:T(8,128)(2,1)}, bf16[1,128,128]{2,1,0:T(8,128)(2,1)}, f32[128,256]{1,0:T(8,128)}) custom-call(bf16[1,128,256]{2,1,0:T(8,128)(2,1)} %get-tuple-element.6.refs_0_, bf16[1,128,128]{2,1,0:T(8,128)(2,1)} %get-tuple-element.7.refs_1_, f32[128,256]{1,0:T(8,128)} %get-tuple-element.8.refs_2_), custom_call_target="tpu_custom_call" | custom-call | tf_op jit(solution)/shard_map/pallas_call | solution.py:325
